TPU v7x, 32 devices: a whole 2x2x4 slice. The times are simulated.
32 devices in a mesh: parts: 2 (over y), angle: 4 (over z), slab: 2 (over x), tile: 2 (over core).
Axes of the slice: x: 2, y: 2, z: 4, core: 2. Of those that a mesh axis runs over, the one named last changes fastest.
Arguments:
- measured: float32 [4, 4, 32, 128], P('angle', 'tile', ('parts', 'slab')), parts along dimension 2, may hold values from -6 to 6
- x_start: float32 [16, 32, 128], P(('angle', 'tile'), ('parts', 'slab')), parts along dimension 1, may hold values from -6 to 6
- block_pixel: int32 [4, 64], P('angle', 'tile'), may hold values from 0 to 15
- block_det: int32 [4, 64], P('angle', 'tile'), may hold values from 0 to 1
- block_count: int32 [4, 2], P('angle', 'tile'), may hold values from 8 to 32, as said below
- interp: bfloat16 [4, 64, 128, 128], P('angle', 'tile'), may hold values from -0.1875 to 0.1875
- lift_gain: float32 [64], replicated, may hold values from -4 to 4
- lift_bias: float32 [64], replicated, may hold values from -3 to 3
- conv_in: bfloat16 [4, 27, 32, 64], replicated, may hold values from -0.21875 to 0.21875
- conv_bias: float32 [4, 64], replicated, may hold values from -3 to 3
- conv_out: bfloat16 [4, 64, 32], replicated, may hold values from -0.75 to 0.75
- out_gain: float32 [64], replicated, may hold values from -0.75 to 0.75
Outputs:
- estimate: float32 [16, 32, 128], P(('angle', 'tile'), ('parts', 'slab')), parts along dimension 1
- denoised: float32 [16, 32, 128], P(('angle', 'tile'), ('parts', 'slab')), parts along dimension 1
There are 2 independent parts, one for each index of `parts`. A program takes and returns all parts, laid end to end along the dimension named above; an argument that names none is the same for every part. Nothing has to cross between parts.
Inputs may be any that keep to these rules, and one draw needn't show every extreme that they name: `block_count`: slots of an angle and detector half at or past its count hold no block. Some angle and half has all 32 slots live.
All inputs are finite; a program needn't handle non-finite values.
Results may differ from a plain program's by a relative error of at most 0.015.
Values may be sent and summed in bfloat16 or wider, within the bound.
A program may use at most 64 MiB of HBM per device.

v0:
```python
import jax
import jax.numpy as jnp
from jax import lax
from jax.experimental import pallas as pl
from jax.experimental.pallas import tpu as pltpu
from jax.sharding import PartitionSpec as P

ITERS = 2
STEP = 0.2
RHO = 0.5
REACH = 2
F32 = jnp.float32
BF16 = jnp.bfloat16
MESH = pl.DeviceIdType.MESH


def kernel(
    group,
    tiles,
    slabs,
    layers,
    channels,
    pixel_ref,
    det_ref,
    count_ref,
    measured_ref,
    start_ref,
    interp_ref,
    conv_in_ref,
    conv_out_ref,
    columns_ref,
    estimate_ref,
    denoised_ref,
    volume,
    volume_rows,
    lhs,
    smeared,
    partial,
    arrived,
    halo,
    weights,
    weights_out,
    features,
    taps,
    products,
    gather_send,
    gather_recv,
    sum_send,
    sum_recv,
    halo_send,
    halo_recv,
):
    half = channels // 2
    part = lax.axis_index("parts")
    slab = lax.axis_index("slab")
    me = lax.axis_index("angle") * tiles + lax.axis_index("tile")
    slots = interp_ref.shape[0] // 128

    def device(member, at_slab):
        return (part, member // tiles, at_slab, lax.rem(member, tiles))

    offsets = [
        (ds, dg) for ds in (-1, 0, 1) for dg in range(-REACH, REACH + 1) if (ds, dg) != (0, 0)
    ]

    def present(ds, dg):
        return jnp.logical_and(
            jnp.logical_and(me + dg >= 0, me + dg < group),
            jnp.logical_and(slab + ds >= 0, slab + ds < slabs),
        )

    def partners(body):
        def step(k, carry):
            body(lax.rem(me + k, group))
            return carry

        lax.fori_loop(1, group, step, 0)

    def neighbours(body):
        for ds, dg in offsets:
            pl.when(present(ds, dg))(lambda ds=ds, dg=dg: body(ds, dg))

    halo[...] = jnp.zeros_like(halo)

    barrier = pltpu.get_barrier_semaphore()
    partners(
        lambda other: pl.semaphore_signal(
            barrier, inc=1, device_id=device(other, slab), device_id_type=MESH
        )
    )
    greeted = group - 1
    for ds, dg in offsets:
        if ds == 0:
            continue

        def greet(ds=ds, dg=dg):
            pl.semaphore_signal(
                barrier, inc=1, device_id=device(me + dg, slab + ds), device_id_type=MESH
            )

        pl.when(present(ds, dg))(greet)
        greeted = greeted + present(ds, dg).astype(jnp.int32)
    pl.semaphore_wait(barrier, greeted)

    def gather_copy(turn, other, owner):
        return pltpu.make_async_remote_copy(
            src_ref=volume.at[turn, me],
            dst_ref=volume.at[turn, owner],
            send_sem=gather_send.at[turn, other],
            recv_sem=gather_recv.at[turn, owner],
            device_id=device(other, slab),
            device_id_type=MESH,
        )

    def gather_start(turn, block):
        volume[turn, me] = block.astype(BF16)
        partners(lambda other: gather_copy(turn, other, me).start())

    def gather_wait(turn):
        def wait(other):
            gather_copy(turn, other, other).wait_recv()
            gather_copy(turn, other, other).wait_send()

        partners(wait)

    def sum_copy(turn, other, owner):
        return pltpu.make_async_remote_copy(
            src_ref=partial.at[turn, other],
            dst_ref=arrived.at[turn, owner],
            send_sem=sum_send.at[turn, other],
            recv_sem=sum_recv.at[turn, owner],
            device_id=device(other, slab),
            device_id_type=MESH,
        )

    def sum_finish(turn):
        def step(k, total):
            other = lax.rem(me + k, group)
            sum_copy(turn, other, other).wait_recv()
            sum_copy(turn, other, other).wait_send()
            return total + arrived[turn, other]

        return lax.fori_loop(1, group, step, partial[turn, me])

    def halo_copy(turn, ds, dg, send):
        place = (1 - ds) * (2 * REACH + 1) + REACH - dg
        if not send:
            place = (1 + ds) * (2 * REACH + 1) + REACH + dg
        sent_place = (1 + ds) * (2 * REACH + 1) + REACH + dg
        return pltpu.make_async_remote_copy(
            src_ref=halo.at[turn, 3 * REACH + 1],
            dst_ref=halo.at[turn, place],
            send_sem=halo_send.at[turn, sent_place],
            recv_sem=halo_recv.at[turn, place],
            device_id=device(me + dg, slab + ds),
            device_id_type=MESH,
        )

    def halo_start(turn, block):
        halo[turn, 3 * REACH + 1] = block
        neighbours(lambda ds, dg: halo_copy(turn, ds, dg, True).start())

    def halo_wait(turn):
        def wait(ds, dg):
            halo_copy(turn, ds, dg, False).wait_recv()
            halo_copy(turn, ds, dg, False).wait_send()

        neighbours(wait)

    def data_step(turn):
        def widen(member, carry):
            volume_rows[pl.ds(2 * member, 2)] = (
                volume[turn, member].astype(F32).reshape(2, 8, 128)
            )
            return carry

        lax.fori_loop(0, group, widen, 0)
        live = [(count_ref[0, 0] > s).astype(F32) for s in range(slots)]
        first = [
            jnp.where(det_ref[0, s] == 0, F32(1.0), F32(0.0)) * live[s] for s in range(slots)
        ]
        second = [
            jnp.where(det_ref[0, s] == 1, F32(1.0), F32(0.0)) * live[s] for s in range(slots)
        ]
        for s in range(slots):
            row = volume_rows[pixel_ref[0, s]]
            lhs[:, 128 * s : 128 * (s + 1)] = jnp.concatenate(
                [row * first[s], row * second[s]], axis=0
            ).astype(BF16)
        projected = jnp.dot(lhs[...], interp_ref[...], preferred_element_type=F32)
        misfit = (projected - measured_ref[...]).astype(BF16)
        for s in range(0, slots, 2):
            both = lax.dot_general(
                misfit,
                interp_ref[128 * s : 128 * (s + 2), :],
                (((1,), (1,)), ((), ())),
                preferred_element_type=F32,
            )
            for k in range(2):
                block = both[:, 128 * k : 128 * (k + 1)]
                smeared[s + k] = block[:8] * first[s + k] + block[8:] * second[s + k]

        def rows_of(owner, carry):
            totals = [jnp.zeros((8, 128), F32) for _ in range(8)]
            for s in range(slots):
                at = jnp.full((8, 128), pixel_ref[0, s], jnp.int32) - 8 * owner
                block = smeared[s]
                for k in range(8):
                    totals[k] = totals[k] + jnp.where(at == k, block, 0.0)
            for k in range(4):
                partial[turn, 4 * owner + k] = jnp.concatenate(
                    totals[2 * k : 2 * k + 2], axis=0
                )
            return carry

        lax.fori_loop(0, group // 4, rows_of, 0)
        partners(lambda other: sum_copy(turn, other, me).start())

    def prepare_weights():
        for layer in range(layers):
            for oz in range(3):
                stacked = jnp.concatenate(
                    [
                        conv_in_ref[layer, 9 * ox + 3 * oz + oy]
                        for ox in range(3)
                        for oy in range(3)
                    ],
                    axis=0,
                )
                weights[layer, channels * oz : channels * (oz + 1), :] = (
                    stacked.astype(F32).T.astype(BF16)
                )
            weights_out[layer] = conv_out_ref[layer].astype(F32).T.astype(BF16)

    def column(index):
        return columns_ref[channels * index : channels * (index + 1), :]

    rows = 2 + 4 * REACH
    depth = 8 + 2 * layers
    lanes = lax.broadcasted_iota(jnp.int32, (half, 128), 1)

    def denoise(turn):
        gain, bias = column(0), column(1)

        def lift(i, carry):
            block, low = i // 2, 8 * lax.rem(i, 2)
            above = halo[turn, block, pl.ds(pl.multiple_of(low, 8), 8), :]
            here = halo[turn, 2 * REACH + 1 + block, pl.ds(pl.multiple_of(low, 8), 8), :]
            below = halo[turn, 4 * REACH + 2 + block, pl.ds(pl.multiple_of(low, 8), 8), :]
            line = jnp.concatenate([above[8 - layers :], here, below[:layers]], axis=0)
            for j in range(depth):
                features[i, j] = gain * line[j : j + 1, :] + bias
            return carry

        lax.fori_loop(0, rows, lift, 0)

        for layer in range(layers):
            active, passive = (0, half) if layer % 2 == 0 else (half, 0)

            def spread(i, carry):
                row = 2 * me - 2 * REACH + i
                row_in = jnp.logical_and(row >= 0, row < 2 * group)
                for j in range(layer, depth - layer):
                    at = 8 * slab - layers + j
                    inside = jnp.logical_and(row_in, jnp.logical_and(at >= 0, at < 8 * slabs))
                    block = features[i, j, active : active + half, :] * inside.astype(F32)
                    before = jnp.where(lanes == 0, 0.0, pltpu.roll(block, 1, 1))
                    after = jnp.where(lanes == 127, 0.0, pltpu.roll(block, 127, 1))
                    taps[j, i] = jnp.concatenate([before, block, after], axis=0).astype(BF16)
                return carry

            lax.fori_loop(layer, rows - layer, spread, 0)
            bias_wide = jnp.concatenate([column(3 + layer)] * 2, axis=1)

            def multiply(r, j):
                left = taps[j, pl.ds(r - 1, 3)].reshape(9 * half, 128)
                right = taps[j, pl.ds(r, 3)].reshape(9 * half, 128)
                products[j] = jnp.dot(
                    weights[layer],
                    jnp.concatenate([left, right], axis=1),
                    preferred_element_type=F32,
                )

            def finish(r, j):
                total = (
                    products[j - 1, :channels]
                    + products[j, channels : 2 * channels]
                    + products[j + 1, 2 * channels :]
                    + bias_wide
                )
                inner = (total / (1.0 + jnp.exp(-total))).astype(BF16)
                change = jnp.dot(weights_out[layer], inner, preferred_element_type=F32)
                features[r, j, passive : passive + half, :] += change[:, :128]
                features[r + 1, j, passive : passive + half, :] += change[:, 128:]

            def pair(index, carry):
                r = layer + 1 + 2 * index
                low, high = layer + 1, depth - layer - 1
                for j in (low - 1, low, low + 1):
                    multiply(r, j)

                def along(j, carry):
                    finish(r, j - 2)
                    multiply(r, j)
                    return carry

                lax.fori_loop(low + 2, high + 1, along, 0)
                finish(r, high - 1)
                return carry

            lax.fori_loop(0, rows // 2 - 1 - layer, pair, 0)

        readout = column(2)
        lines = []
        for i in range(2):
            for j in range(8):
                lines.append(
                    jnp.sum(
                        features[2 * REACH + i, layers + j] * readout, axis=0, keepdims=True
                    )
                )
        return halo[turn, 3 * REACH + 1] + jnp.concatenate(lines, axis=0)

    estimate = start_ref[...]
    denoised = estimate
    scaled_dual = jnp.zeros_like(estimate)
    gather_start(0, estimate)
    prepare_weights()
    gather_wait(0)
    data_step(0)
    for turn in range(ITERS):
        gradient = sum_finish(turn)
        estimate = estimate - STEP * (gradient + RHO * (estimate - denoised + scaled_dual))
        if turn + 1 == ITERS:
            estimate_ref[...] = estimate
        halo_start(turn, estimate + scaled_dual)
        if turn + 1 < ITERS:
            gather_start(turn + 1, estimate)
            gather_wait(turn + 1)
            data_step(turn + 1)
        halo_wait(turn)
        fresh = denoise(turn)
        if turn + 1 < ITERS:
            scaled_dual = scaled_dual + estimate - fresh
        denoised = fresh
    denoised_ref[...] = denoised


def solution(mesh):
    in_specs = (
        P("angle", "tile", ("parts", "slab"), None),
        P(("angle", "tile"), ("parts", "slab"), None),
        P("angle", "tile"),
        P("angle", "tile"),
        P("angle", "tile"),
        P("angle", "tile", None, None),
        P(),
        P(),
        P(),
        P(),
        P(),
        P(),
    )
    out_specs = (
        P(("angle", "tile"), ("parts", "slab"), None),
        P(("angle", "tile"), ("parts", "slab"), None),
    )
    tiles = mesh.shape["tile"]
    group = mesh.shape["angle"] * tiles
    slabs = mesh.shape["slab"]

    def local(
        measured,
        x_start,
        block_pixel,
        block_det,
        block_count,
        interp,
        lift_gain,
        lift_bias,
        conv_in,
        conv_bias,
        conv_out,
        out_gain,
    ):
        channels = lift_gain.shape[0]
        layers = conv_in.shape[0]
        slots = interp.shape[1]
        half = channels // 2
        rows, depth = 2 + 4 * REACH, 8 + 2 * layers
        columns = jnp.concatenate([lift_gain, lift_bias, out_gain, conv_bias.reshape(-1)])
        columns = jnp.broadcast_to(columns[:, None], (columns.shape[0], 128))
        vmem = pl.BlockSpec(memory_space=pltpu.VMEM)
        smem = pl.BlockSpec(memory_space=pltpu.SMEM)
        places = 3 * (2 * REACH + 1)

        def run(*refs):
            kernel(group, tiles, slabs, layers, channels, *refs)

        estimate, denoised = pl.pallas_call(
            run,
            out_shape=[jax.ShapeDtypeStruct((16, 128), F32)] * 2,
            in_specs=[smem] * 3 + [vmem] * 6,
            out_specs=[vmem] * 2,
            scratch_shapes=[
                pltpu.VMEM((ITERS, group, 16, 128), BF16),
                pltpu.VMEM((2 * group, 8, 128), F32),
                pltpu.VMEM((16, 128 * slots), BF16),
                pltpu.VMEM((slots, 8, 128), F32),
                pltpu.VMEM((ITERS, group, 16, 128), F32),
                pltpu.VMEM((ITERS, group, 16, 128), F32),
                pltpu.VMEM((ITERS, places, 16, 128), F32),
                pltpu.VMEM((layers, 3 * channels, 9 * half), BF16),
                pltpu.VMEM((layers, half, channels), BF16),
                pltpu.VMEM((rows, depth, channels, 128), F32),
                pltpu.VMEM((depth, rows, 3 * half, 128), BF16),
                pltpu.VMEM((depth, 3 * channels, 256), F32),
                pltpu.SemaphoreType.DMA((ITERS, group)),
                pltpu.SemaphoreType.DMA((ITERS, group)),
                pltpu.SemaphoreType.DMA((ITERS, group)),
                pltpu.SemaphoreType.DMA((ITERS, group)),
                pltpu.SemaphoreType.DMA((ITERS, places)),
                pltpu.SemaphoreType.DMA((ITERS, places)),
            ],
            compiler_params=pltpu.CompilerParams(
                collective_id=0, has_side_effects=True, vmem_limit_bytes=48 * 1024 * 1024
            ),
        )(
            block_pixel,
            block_det,
            block_count,
            measured.reshape(16, 128),
            x_start.reshape(16, 128),
            interp.reshape(slots * 128, 128),
            conv_in,
            conv_out,
            columns,
        )
        return estimate.reshape(2, 8, 128), denoised.reshape(2, 8, 128)

    return jax.shard_map(local, mesh=mesh, in_specs=in_specs, out_specs=out_specs, check_vma=False)
```

profile of v0, /device:TPU:0, one launch (start us, length us, event | category | flops | bytes accessed | tf_op | source)
XLA Modules:
  0.0 99.4 jit_solution(7688591884626189696)
XLA Ops:
  1.3 0.0 copy-start.6
  1.3 0.7 copy-done.6
  2.0 0.0 copy-start.7
  2.0 0.0 copy-start.8
  2.0 0.0 copy-start.9
  2.0 0.1 reshape.26
  2.0 0.6 copy-done.7
  2.6 0.0 copy-done.8
  2.6 0.0 copy-done.9
  2.6 0.1 pad_maximum_fusion
  2.7 0.9 copy.14.refs_7_
  3.6 0.0 copy-start.2
  3.6 0.0 copy-start.3
  3.6 0.0 copy-start.4
  3.6 0.0 copy-start.5
  3.6 0.1 broadcast_in_dim.2.refs_8_
  3.7 0.5 copy-done.2
  4.3 0.0 copy-done.3
  4.3 0.0 copy-done.4
  4.3 0.0 copy-done.5
  4.3 0.0 copy-start
  4.3 1.2 %copy-done = bf16[1,32,128,128]{3,2,1,0:T(8,128)(2,1)S(1)} copy-done((bf16[1,32,128,128]{3,2,1,0:T(8,128)(2,1)S(1)}, bf16[1,32,128,128]{3,2,1,0:T(8,128)(2,1)}, u32[]{:S(2)}) %copy-start) | copy-done | bytes 1048600
  5.5 0.0 copy-start.1
  5.5 1.2 %copy-done.1 = bf16[4,27,32,64]{3,2,1,0:T(8,128)(2,1)S(1)} copy-done((bf16[4,27,32,64]{3,2,1,0:T(8,128)(2,1)S(1)}, bf16[4,27,32,64]{3,2,1,0:T(8,128)(2,1)}, u32[]{:S(2)}) %copy-start.1) | copy-done | bytes 442392
  6.7 91.5 %shard_map.131 = (f32[16,128]{1,0:T(8,128)S(1)}, f32[16,128]{1,0:T(8,128)S(1)}) custom-call(s32[1,32]{1,0:T(1,128)S(1)} %copy-done.4, s32[1,32]{1,0:T(1,128)S(1)} %copy-done.5, s32[1,1]{1,0:T(1,128)S(6)} %copy.17.refs_2_, f32[16,128]{1,0:T(8,128)S(1)} %bitcast.6, f32[16,128]{1,0:T(8,128)S(1)} %bitcast.7, bf16[4096,128]{1,0:T(8,128)(2,1)S(1)} %bitcast.5, ...), custom_call_target="tpu_custom_call" | custom-call | tf_op jit(solution)/shard_map/pallas_call | solution.py:400
  98.2 0.6 copy.18
  98.8 0.6 copy.19
Async XLA Ops:
  1.3 0.7 copy-start.6
  2.0 0.7 copy-start.7
  2.0 0.7 copy-start.8
  2.0 0.7 copy-start.9
  3.6 0.7 copy-start.2
  3.6 0.7 copy-start.3
  3.6 0.7 copy-start.4
  3.6 0.7 copy-start.5
  4.3 1.2 %copy-start = (bf16[1,32,128,128]{3,2,1,0:T(8,128)(2,1)S(1)}, bf16[1,32,128,128]{3,2,1,0:T(8,128)(2,1)}, u32[]{:S(2)}) copy-start(bf16[1,32,128,128]{3,2,1,0:T(8,128)(2,1)} %param.17) | copy-start | bytes 3145732
  5.5 1.2 %copy-start.1 = (bf16[4,27,32,64]{3,2,1,0:T(8,128)(2,1)S(1)}, bf16[4,27,32,64]{3,2,1,0:T(8,128)(2,1)}, u32[]{:S(2)}) copy-start(bf16[4,27,32,64]{3,2,1,0:T(8,128)(2,1)} %refs_6_.1) | copy-start | bytes 1327108
where the time goes:
time: 99.8 us; the launch traced here: 99.4 us
  Pallas kernels  91.5 us (92%)
  local copies, waits for them, and re-layouts  6.49 us (7%)
  between operations  1.34 us (1%)
    pallas_call x1, Pallas kernels, local(): pl.pallas_call(run, out_shape=[jax.ShapeDtypeStruct((16, 128), F32)] * 2,...  91.5 us
    unnamed x23, local copies, waits for them, and re-layouts  6.29 us

commit v1 on v0

--- a/solution.py
+++ b/solution.py
@@ -20,17 +20,33 @@
     slabs,
     layers,
     channels,
+    pixel_in,
+    det_in,
+    count_in,
+    start_in,
+    measured_in,
+    interp_in,
+    conv_in_in,
+    conv_out_in,
+    gain_in,
+    bias_in,
+    readout_in,
+    conv_bias_in,
+    estimate_ref,
+    denoised_ref,
     pixel_ref,
     det_ref,
     count_ref,
+    start_ref,
     measured_ref,
-    start_ref,
     interp_ref,
     conv_in_ref,
     conv_out_ref,
+    gain_ref,
+    bias_ref,
+    readout_ref,
+    conv_bias_ref,
     columns_ref,
-    estimate_ref,
-    denoised_ref,
     volume,
     volume_rows,
     lhs,
@@ -41,8 +57,10 @@
     weights,
     weights_out,
     features,
-    taps,
+    taps_even,
+    taps_odd,
     products,
+    input_sems,
     gather_send,
     gather_recv,
     sum_send,
@@ -80,7 +98,67 @@
         for ds, dg in offsets:
             pl.when(present(ds, dg))(lambda ds=ds, dg=dg: body(ds, dg))
 
+    loads = [
+        pltpu.make_async_copy(source, target, input_sems.at[index])
+        for index, (source, target) in enumerate(
+            [
+                (start_in, start_ref),
+                (gain_in, gain_ref),
+                (bias_in, bias_ref),
+                (readout_in, readout_ref),
+                (conv_bias_in, conv_bias_ref),
+                (conv_in_in, conv_in_ref),
+                (conv_out_in, conv_out_ref),
+                (interp_in, interp_ref),
+                (pixel_in, pixel_ref),
+                (det_in, det_ref),
+                (count_in, count_ref),
+                (measured_in, measured_ref),
+            ]
+        )
+    ]
+    for load in loads:
+        load.start()
     halo[...] = jnp.zeros_like(halo)
+    rows = 2 + 4 * REACH
+    if slabs == 2:
+        depth = 10 + layers
+        base = slab * (8 - layers) - 1
+        own = slab * layers + 1
+    else:
+        depth = 8 + 2 * layers
+        base = 8 * slab - layers
+        own = layers
+    for ref in (taps_even, taps_odd):
+        ref[0] = jnp.zeros(ref.shape[1:], BF16)
+        ref[depth - 1] = jnp.zeros(ref.shape[1:], BF16)
+
+    def prepare_weights():
+        for layer in range(layers):
+            for oz in range(3):
+                stacked = jnp.concatenate(
+                    [
+                        conv_in_ref[layer, 9 * ox + 3 * oz + oy]
+                        for ox in range(3)
+                        for oy in range(3)
+                    ],
+                    axis=0,
+                )
+                weights[layer, channels * oz : channels * (oz + 1), :] = (
+                    stacked.astype(F32).T.astype(BF16)
+                )
+            wide = jnp.concatenate([conv_out_ref[layer].astype(F32)] * 4, axis=1)
+            place = lax.broadcasted_iota(jnp.int32, wide.shape, 1) // channels
+            for k in range(4):
+                weights_out[layer, half * k : half * (k + 1), :] = jnp.where(
+                    place == k, wide, 0.0
+                ).astype(BF16)
+        vectors = [gain_ref[...], bias_ref[...], readout_ref[...]]
+        vectors += [conv_bias_ref[layer : layer + 1, :] for layer in range(layers)]
+        for index, vector in enumerate(vectors):
+            columns_ref[channels * index : channels * (index + 1), :] = jnp.broadcast_to(
+                vector, (128, channels)
+            ).T
 
     barrier = pltpu.get_barrier_semaphore()
     partners(
@@ -100,6 +178,9 @@
 
         pl.when(present(ds, dg))(greet)
         greeted = greeted + present(ds, dg).astype(jnp.int32)
+    for load in loads[:7]:
+        load.wait()
+    prepare_weights()
     pl.semaphore_wait(barrier, greeted)
 
     def gather_copy(turn, other, owner):
@@ -138,9 +219,9 @@
             other = lax.rem(me + k, group)
             sum_copy(turn, other, other).wait_recv()
             sum_copy(turn, other, other).wait_send()
-            return total + arrived[turn, other]
-
-        return lax.fori_loop(1, group, step, partial[turn, me])
+            return total + arrived[turn, other].astype(F32)
+
+        return lax.fori_loop(1, group, step, partial[turn, me].astype(F32))
 
     def halo_copy(turn, ds, dg, send):
         place = (1 - ds) * (2 * REACH + 1) + REACH - dg
@@ -210,36 +291,32 @@
             for k in range(4):
                 partial[turn, 4 * owner + k] = jnp.concatenate(
                     totals[2 * k : 2 * k + 2], axis=0
-                )
+                ).astype(BF16)
             return carry
 
         lax.fori_loop(0, group // 4, rows_of, 0)
         partners(lambda other: sum_copy(turn, other, me).start())
 
-    def prepare_weights():
-        for layer in range(layers):
-            for oz in range(3):
-                stacked = jnp.concatenate(
-                    [
-                        conv_in_ref[layer, 9 * ox + 3 * oz + oy]
-                        for ox in range(3)
-                        for oy in range(3)
-                    ],
-                    axis=0,
-                )
-                weights[layer, channels * oz : channels * (oz + 1), :] = (
-                    stacked.astype(F32).T.astype(BF16)
-                )
-            weights_out[layer] = conv_out_ref[layer].astype(F32).T.astype(BF16)
-
     def column(index):
         return columns_ref[channels * index : channels * (index + 1), :]
 
-    rows = 2 + 4 * REACH
-    depth = 8 + 2 * layers
     lanes = lax.broadcasted_iota(jnp.int32, (half, 128), 1)
 
-    def denoise(turn):
+    def inside(i, j):
+        row = 2 * me - 2 * REACH + i
+        within = jnp.logical_and(row >= 0, row < 2 * group)
+        if slabs != 2:
+            at = base + j
+            within = jnp.logical_and(within, jnp.logical_and(at >= 0, at < 8 * slabs))
+        return within.astype(F32)
+
+    def put_taps(target, i, j, block):
+        block = block * inside(i, j)
+        before = jnp.where(lanes == 0, 0.0, pltpu.roll(block, 1, 1))
+        after = jnp.where(lanes == 127, 0.0, pltpu.roll(block, 127, 1))
+        target[j, i] = jnp.concatenate([before, block, after], axis=0).astype(BF16)
+
+    def denoise(turn, between):
         gain, bias = column(0), column(1)
 
         def lift(i, carry):
@@ -247,77 +324,106 @@
             above = halo[turn, block, pl.ds(pl.multiple_of(low, 8), 8), :]
             here = halo[turn, 2 * REACH + 1 + block, pl.ds(pl.multiple_of(low, 8), 8), :]
             below = halo[turn, 4 * REACH + 2 + block, pl.ds(pl.multiple_of(low, 8), 8), :]
-            line = jnp.concatenate([above[8 - layers :], here, below[:layers]], axis=0)
-            for j in range(depth):
-                features[i, j] = gain * line[j : j + 1, :] + bias
+            if slabs == 2:
+                line = jnp.where(
+                    slab == 0,
+                    jnp.concatenate([here, below[:layers]], axis=0),
+                    jnp.concatenate([above[8 - layers :], here], axis=0),
+                )
+                first = 1
+            else:
+                line = jnp.concatenate([above[8 - layers :], here, below[:layers]], axis=0)
+                first = 0
+            for j in range(line.shape[0]):
+                block = gain * line[j : j + 1, :] + bias
+                features[i, first + j] = block
+                put_taps(taps_even, i, first + j, block[:half])
             return carry
 
         lax.fori_loop(0, rows, lift, 0)
 
         for layer in range(layers):
-            active, passive = (0, half) if layer % 2 == 0 else (half, 0)
-
-            def spread(i, carry):
-                row = 2 * me - 2 * REACH + i
-                row_in = jnp.logical_and(row >= 0, row < 2 * group)
-                for j in range(layer, depth - layer):
-                    at = 8 * slab - layers + j
-                    inside = jnp.logical_and(row_in, jnp.logical_and(at >= 0, at < 8 * slabs))
-                    block = features[i, j, active : active + half, :] * inside.astype(F32)
-                    before = jnp.where(lanes == 0, 0.0, pltpu.roll(block, 1, 1))
-                    after = jnp.where(lanes == 127, 0.0, pltpu.roll(block, 127, 1))
-                    taps[j, i] = jnp.concatenate([before, block, after], axis=0).astype(BF16)
-                return carry
-
-            lax.fori_loop(layer, rows - layer, spread, 0)
+            passive = half if layer % 2 == 0 else 0
+            taps, taps_next = (
+                (taps_even, taps_odd) if layer % 2 == 0 else (taps_odd, taps_even)
+            )
             bias_wide = jnp.concatenate([column(3 + layer)] * 2, axis=1)
-
-            def multiply(r, j):
-                left = taps[j, pl.ds(r - 1, 3)].reshape(9 * half, 128)
-                right = taps[j, pl.ds(r, 3)].reshape(9 * half, 128)
-                products[j] = jnp.dot(
+            pairs = rows // 2 - 1 - layer
+            if slabs == 2:
+                low, count = 1 + slab * (1 + layer), 7 + layers - layer
+            else:
+                low, count = 1 + layer, 6 + 2 * layers - 2 * layer
+            unroll = min(u for u in range(1, count + 1) if count % u == 0 and u * pairs >= 4)
+
+            def multiply(p, j):
+                r = layer + 1 + 2 * p
+                left = taps[j, r - 1 : r + 2].reshape(9 * half, 128)
+                right = taps[j, r : r + 3].reshape(9 * half, 128)
+                products[p, j] = jnp.dot(
                     weights[layer],
                     jnp.concatenate([left, right], axis=1),
                     preferred_element_type=F32,
                 )
 
-            def finish(r, j):
+            def activate(p, j):
                 total = (
-                    products[j - 1, :channels]
-                    + products[j, channels : 2 * channels]
-                    + products[j + 1, 2 * channels :]
+                    products[p, j - 1, :channels]
+                    + products[p, j, channels : 2 * channels]
+                    + products[p, j + 1, 2 * channels :]
                     + bias_wide
                 )
-                inner = (total / (1.0 + jnp.exp(-total))).astype(BF16)
-                change = jnp.dot(weights_out[layer], inner, preferred_element_type=F32)
-                features[r, j, passive : passive + half, :] += change[:, :128]
-                features[r + 1, j, passive : passive + half, :] += change[:, 128:]
-
-            def pair(index, carry):
-                r = layer + 1 + 2 * index
-                low, high = layer + 1, depth - layer - 1
-                for j in (low - 1, low, low + 1):
-                    multiply(r, j)
-
-                def along(j, carry):
-                    finish(r, j - 2)
-                    multiply(r, j)
-                    return carry
-
-                lax.fori_loop(low + 2, high + 1, along, 0)
-                finish(r, high - 1)
+                return (total / (1.0 + jnp.exp(-total))).astype(BF16)
+
+            def add(p, j, change):
+                r = layer + 1 + 2 * p
+                for k in range(2):
+                    block = (
+                        features[r + k, j, passive : passive + half, :]
+                        + change[:, 128 * k : 128 * (k + 1)]
+                    )
+                    features[r + k, j, passive : passive + half, :] = block
+                    if layer + 1 < layers:
+                        put_taps(taps_next, r + k, j, block)
+
+            def several(j, number):
+                return [(p, j + k) for k in range(number) for p in range(pairs)]
+
+            def finish(j):
+                items = several(j, unroll)
+                for at in range(0, len(items), 4):
+                    some = items[at : at + 4]
+                    inner = jnp.concatenate([activate(*item) for item in some], axis=0)
+                    change = jnp.dot(
+                        weights_out[layer, : half * len(some), : channels * len(some)],
+                        inner,
+                        preferred_element_type=F32,
+                    )
+                    for k, item in enumerate(some):
+                        add(*item, change[half * k : half * (k + 1)])
+
+            def begin(t, carry):
+                for item in several(low - 1 + t, 1):
+                    multiply(*item)
                 return carry
 
-            lax.fori_loop(0, rows // 2 - 1 - layer, pair, 0)
+            def along(t, carry):
+                finish(low + unroll * t)
+                for item in several(low + 1 + unroll * (t + 1), unroll):
+                    multiply(*item)
+                return carry
+
+            lax.fori_loop(0, unroll + 2, begin, 0)
+            lax.fori_loop(0, count // unroll - 1, along, 0)
+            finish(low + count - unroll)
+            if layer == 0:
+                between()
 
         readout = column(2)
         lines = []
         for i in range(2):
             for j in range(8):
                 lines.append(
-                    jnp.sum(
-                        features[2 * REACH + i, layers + j] * readout, axis=0, keepdims=True
-                    )
+                    jnp.sum(features[2 * REACH + i, own + j] * readout, axis=0, keepdims=True)
                 )
         return halo[turn, 3 * REACH + 1] + jnp.concatenate(lines, axis=0)
 
@@ -325,8 +431,9 @@
     denoised = estimate
     scaled_dual = jnp.zeros_like(estimate)
     gather_start(0, estimate)
-    prepare_weights()
     gather_wait(0)
+    for load in loads[7:]:
+        load.wait()
     data_step(0)
     for turn in range(ITERS):
         gradient = sum_finish(turn)
@@ -336,10 +443,14 @@
         halo_start(turn, estimate + scaled_dual)
         if turn + 1 < ITERS:
             gather_start(turn + 1, estimate)
-            gather_wait(turn + 1)
-            data_step(turn + 1)
         halo_wait(turn)
-        fresh = denoise(turn)
+
+        def between(turn=turn):
+            if turn + 1 < ITERS:
+                gather_wait(turn + 1)
+                data_step(turn + 1)
+
+        fresh = denoise(turn, between)
         if turn + 1 < ITERS:
             scaled_dual = scaled_dual + estimate - fresh
         denoised = fresh
@@ -387,11 +498,10 @@
         layers = conv_in.shape[0]
         slots = interp.shape[1]
         half = channels // 2
-        rows, depth = 2 + 4 * REACH, 8 + 2 * layers
-        columns = jnp.concatenate([lift_gain, lift_bias, out_gain, conv_bias.reshape(-1)])
-        columns = jnp.broadcast_to(columns[:, None], (columns.shape[0], 128))
+        rows = 2 + 4 * REACH
+        depth = 10 + layers if slabs == 2 else 8 + 2 * layers
         vmem = pl.BlockSpec(memory_space=pltpu.VMEM)
-        smem = pl.BlockSpec(memory_space=pltpu.SMEM)
+        hbm = pl.BlockSpec(memory_space=pltpu.HBM)
         places = 3 * (2 * REACH + 1)
 
         def run(*refs):
@@ -400,21 +510,36 @@
         estimate, denoised = pl.pallas_call(
             run,
             out_shape=[jax.ShapeDtypeStruct((16, 128), F32)] * 2,
-            in_specs=[smem] * 3 + [vmem] * 6,
+            in_specs=[hbm] * 12,
             out_specs=[vmem] * 2,
             scratch_shapes=[
+                pltpu.SMEM(block_pixel.shape, jnp.int32),
+                pltpu.SMEM(block_det.shape, jnp.int32),
+                pltpu.SMEM(block_count.shape, jnp.int32),
+                pltpu.VMEM((16, 128), F32),
+                pltpu.VMEM((16, 128), F32),
+                pltpu.VMEM((slots * 128, 128), BF16),
+                pltpu.VMEM(conv_in.shape, BF16),
+                pltpu.VMEM((layers, half, channels), BF16),
+                pltpu.VMEM((1, channels), F32),
+                pltpu.VMEM((1, channels), F32),
+                pltpu.VMEM((1, channels), F32),
+                pltpu.VMEM((layers, channels), F32),
+                pltpu.VMEM(((3 + layers) * channels, 128), F32),
                 pltpu.VMEM((ITERS, group, 16, 128), BF16),
                 pltpu.VMEM((2 * group, 8, 128), F32),
                 pltpu.VMEM((16, 128 * slots), BF16),
                 pltpu.VMEM((slots, 8, 128), F32),
-                pltpu.VMEM((ITERS, group, 16, 128), F32),
-                pltpu.VMEM((ITERS, group, 16, 128), F32),
+                pltpu.VMEM((ITERS, group, 16, 128), BF16),
+                pltpu.VMEM((ITERS, group, 16, 128), BF16),
                 pltpu.VMEM((ITERS, places, 16, 128), F32),
                 pltpu.VMEM((layers, 3 * channels, 9 * half), BF16),
-                pltpu.VMEM((layers, half, channels), BF16),
+                pltpu.VMEM((layers, 4 * half, 4 * channels), BF16),
                 pltpu.VMEM((rows, depth, channels, 128), F32),
                 pltpu.VMEM((depth, rows, 3 * half, 128), BF16),
-                pltpu.VMEM((depth, 3 * channels, 256), F32),
+                pltpu.VMEM((depth, rows, 3 * half, 128), BF16),
+                pltpu.VMEM((rows // 2 - 1, depth, 3 * channels, 256), F32),
+                pltpu.SemaphoreType.DMA((12,)),
                 pltpu.SemaphoreType.DMA((ITERS, group)),
                 pltpu.SemaphoreType.DMA((ITERS, group)),
                 pltpu.SemaphoreType.DMA((ITERS, group)),
@@ -429,12 +554,15 @@
             block_pixel,
             block_det,
             block_count,
+            x_start.reshape(16, 128),
             measured.reshape(16, 128),
-            x_start.reshape(16, 128),
             interp.reshape(slots * 128, 128),
             conv_in,
-            conv_out,
-            columns,
+            jnp.swapaxes(conv_out, 1, 2),
+            lift_gain.reshape(1, channels),
+            lift_bias.reshape(1, channels),
+            out_gain.reshape(1, channels),
+            conv_bias,
         )
         return estimate.reshape(2, 8, 128), denoised.reshape(2, 8, 128)
 

time: 99.8 us -> 62.7 us (0.63)
  Pallas kernels: 91.5 us -> 55.3 us
    pallas_call x1, Pallas kernels: 91.5 us -> 55.3 us  [local(): pl.pallas_call(run, out_shape=[jax.ShapeDtypeStruct((16, 128), F32)] * 2,...]
    unnamed x23 -> x24, local copies, waits for them, and re-layouts: 6.29 us -> 5.72 us
where the time goes in v1:
time: 62.7 us; the launch traced here: 62.4 us
  Pallas kernels  55.3 us (88%)
  local copies, waits for them, and re-layouts  5.72 us (9%)
  between operations  1.37 us (2%)
    pallas_call x1, Pallas kernels, local(): pl.pallas_call(run, out_shape=[jax.ShapeDtypeStruct((16, 128), F32)] * 2,...  55.3 us
    unnamed x24, local copies, waits for them, and re-layouts  5.72 us

profile of v1, /device:TPU:0, one launch (start us, length us, event | category | flops | bytes accessed | tf_op | source)
XLA Modules:
  0.0 62.4 jit_solution(17359825529200047959)
XLA Ops:
  0.6 0.0 copy-start.3
  1.3 0.0 copy-start.9
  1.3 0.0 copy-start.10
  1.3 0.0 copy-start.5
  1.3 0.0 copy-start.6
  1.3 0.0 copy-start.7
  1.4 0.0 copy-start.8
  1.4 0.0 copy-done.3
  1.4 0.6 copy-done.9
  2.0 0.0 copy-done.10
  2.0 0.0 copy-done.5
  2.0 0.0 copy-done.6
  2.0 0.0 copy-done.7
  2.0 0.0 copy-done.8
  2.0 0.0 copy-start
  2.0 1.2 %copy-done = bf16[1,32,128,128]{3,2,1,0:T(8,128)(2,1)S(1)} copy-done((bf16[1,32,128,128]{3,2,1,0:T(8,128)(2,1)S(1)}, bf16[1,32,128,128]{3,2,1,0:T(8,128)(2,1)}, u32[]{:S(2)}) %copy-start) | copy-done | bytes 1048600
  3.3 0.0 copy-start.1
  3.3 1.2 %copy-done.1 = bf16[4,27,32,64]{3,2,1,0:T(8,128)(2,1)S(1)} copy-done((bf16[4,27,32,64]{3,2,1,0:T(8,128)(2,1)S(1)}, bf16[4,27,32,64]{3,2,1,0:T(8,128)(2,1)}, u32[]{:S(2)}) %copy-start.1) | copy-done | bytes 442392
  4.4 0.0 copy-start.2
  4.4 0.8 %copy-done.2 = bf16[4,64,32]{1,2,0:T(8,128)(2,1)S(1)} copy-done((bf16[4,64,32]{1,2,0:T(8,128)(2,1)S(1)}, bf16[4,64,32]{1,2,0:T(8,128)(2,1)}, u32[]{:S(2)}) %copy-start.2) | copy-done | bytes 16408
  5.2 0.0 copy-start.4
  5.2 0.7 %copy-done.4 = f32[1,2,8,128]{3,2,1,0:T(8,128)S(1)} copy-done((f32[1,2,8,128]{3,2,1,0:T(8,128)S(1)}, f32[1,2,8,128]{3,2,1,0:T(8,128)}, u32[]{:S(2)}) %copy-start.4) | copy-done | bytes 8216
  5.9 55.3 %shard_map.131 = (f32[16,128]{1,0:T(8,128)S(1)}, f32[16,128]{1,0:T(8,128)S(1)}) custom-call(s32[1,32]{1,0:T(1,128)S(1)} %copy-done.6, s32[1,32]{1,0:T(1,128)S(1)} %copy-done.7, s32[1,1]{1,0:T(1,128)S(6)} %copy.16.refs_2_, f32[16,128]{1,0:T(8,128)S(1)} %bitcast.11, f32[16,128]{1,0:T(8,128)S(1)} %bitcast.12, bf16[4096,128]{1,0:T(8,128)(2,1)S(1)} %bitcast.9, ...), custom_call_target="tpu_custom_call" | custom-call | tf_op jit(solution)/shard_map/pallas_call | solution.py:510
  61.2 0.6 copy.17
  61.8 0.6 copy.18
Async XLA Ops:
  0.6 0.7 %copy-start.3 = (f32[2,8,128]{2,1,0:T(8,128)S(1)}, f32[2,8,128]{2,1,0:T(8,128)}, u32[]{:S(2)}) copy-start(f32[2,8,128]{2,1,0:T(8,128)} %param.13) | copy-start | bytes 24580
  1.3 0.7 %copy-start.9 = (f32[64]{0:T(128)S(1)}, f32[64]{0:T(128)}, u32[]{:S(2)}) copy-start(f32[64]{0:T(128)} %param.19) | copy-start | bytes 772
  1.3 0.7 %copy-start.10 = (f32[64]{0:T(128)S(1)}, f32[64]{0:T(128)}, u32[]{:S(2)}) copy-start(f32[64]{0:T(128)} %param.23) | copy-start | bytes 772
  1.3 0.7 %copy-start.5 = (f32[4,64]{1,0:T(4,128)S(1)}, f32[4,64]{1,0:T(4,128)}, u32[]{:S(2)}) copy-start(f32[4,64]{1,0:T(4,128)} %refs_11_.1) | copy-start | bytes 3076
  1.3 0.7 %copy-start.6 = (s32[1,32]{1,0:T(1,128)S(1)}, s32[1,32]{1,0:T(1,128)}, u32[]{:S(2)}) copy-start(s32[1,32]{1,0:T(1,128)} %refs_0_.1) | copy-start | bytes 388
  1.3 0.7 %copy-start.7 = (s32[1,32]{1,0:T(1,128)S(1)}, s32[1,32]{1,0:T(1,128)}, u32[]{:S(2)}) copy-start(s32[1,32]{1,0:T(1,128)} %refs_1_.1) | copy-start | bytes 388
  1.4 0.7 %copy-start.8 = (f32[64]{0:T(128)S(1)}, f32[64]{0:T(128)}, u32[]{:S(2)}) copy-start(f32[64]{0:T(128)} %param.18) | copy-start | bytes 772
  2.0 1.2 %copy-start = (bf16[1,32,128,128]{3,2,1,0:T(8,128)(2,1)S(1)}, bf16[1,32,128,128]{3,2,1,0:T(8,128)(2,1)}, u32[]{:S(2)}) copy-start(bf16[1,32,128,128]{3,2,1,0:T(8,128)(2,1)} %param.17) | copy-start | bytes 3145732
  3.3 1.2 %copy-start.1 = (bf16[4,27,32,64]{3,2,1,0:T(8,128)(2,1)S(1)}, bf16[4,27,32,64]{3,2,1,0:T(8,128)(2,1)}, u32[]{:S(2)}) copy-start(bf16[4,27,32,64]{3,2,1,0:T(8,128)(2,1)} %refs_6_.1) | copy-start | bytes 1327108
  4.4 0.8 %copy-start.2 = (bf16[4,64,32]{1,2,0:T(8,128)(2,1)S(1)}, bf16[4,64,32]{1,2,0:T(8,128)(2,1)}, u32[]{:S(2)}) copy-start(bf16[4,64,32]{1,2,0:T(8,128)(2,1)} %param.22) | copy-start | bytes 49156
  5.2 0.7 %copy-start.4 = (f32[1,2,8,128]{3,2,1,0:T(8,128)S(1)}, f32[1,2,8,128]{3,2,1,0:T(8,128)}, u32[]{:S(2)}) copy-start(f32[1,2,8,128]{3,2,1,0:T(8,128)} %param.12) | copy-start | bytes 24580

commit v2 on v1

--- a/solution.py
+++ b/solution.py
@@ -92,7 +92,7 @@
             body(lax.rem(me + k, group))
             return carry
 
-        lax.fori_loop(1, group, step, 0)
+        lax.fori_loop(1, group, step, 0, unroll=group <= 8)
 
     def neighbours(body):
         for ds, dg in offsets:
@@ -200,7 +200,6 @@
     def gather_wait(turn):
         def wait(other):
             gather_copy(turn, other, other).wait_recv()
-            gather_copy(turn, other, other).wait_send()
 
         partners(wait)
 
@@ -218,10 +217,9 @@
         def step(k, total):
             other = lax.rem(me + k, group)
             sum_copy(turn, other, other).wait_recv()
-            sum_copy(turn, other, other).wait_send()
             return total + arrived[turn, other].astype(F32)
 
-        return lax.fori_loop(1, group, step, partial[turn, me].astype(F32))
+        return lax.fori_loop(1, group, step, partial[turn, me].astype(F32), unroll=group <= 8)
 
     def halo_copy(turn, ds, dg, send):
         place = (1 - ds) * (2 * REACH + 1) + REACH - dg
@@ -244,9 +242,16 @@
     def halo_wait(turn):
         def wait(ds, dg):
             halo_copy(turn, ds, dg, False).wait_recv()
-            halo_copy(turn, ds, dg, False).wait_send()
 
         neighbours(wait)
+
+    def sends_wait(turn):
+        def wait(other):
+            gather_copy(turn, other, other).wait_send()
+            sum_copy(turn, other, other).wait_send()
+
+        partners(wait)
+        neighbours(lambda ds, dg: halo_copy(turn, ds, dg, False).wait_send())
 
     def data_step(turn):
         def widen(member, carry):
@@ -372,7 +377,8 @@
                     + products[p, j + 1, 2 * channels :]
                     + bias_wide
                 )
-                return (total / (1.0 + jnp.exp(-total))).astype(BF16)
+                total = 0.5 * total
+                return (total + total * jnp.tanh(total)).astype(BF16)
 
             def add(p, j, change):
                 r = layer + 1 + 2 * p
@@ -455,6 +461,8 @@
             scaled_dual = scaled_dual + estimate - fresh
         denoised = fresh
     denoised_ref[...] = denoised
+    for turn in range(ITERS):
+        sends_wait(turn)
 
 
 def solution(mesh):
@@ -548,7 +556,7 @@
                 pltpu.SemaphoreType.DMA((ITERS, places)),
             ],
             compiler_params=pltpu.CompilerParams(
-                collective_id=0, has_side_effects=True, vmem_limit_bytes=48 * 1024 * 1024
+                collective_id=0, has_side_effects=True, vmem_limit_bytes=63 * 1024 * 1024
             ),
         )(
             block_pixel,

time: 62.7 us -> 57.5 us (0.917)
  local copies, waits for them, and re-layouts: 5.72 us -> 1.9 us
  Pallas kernels: 55.3 us -> 54.1 us
    unnamed x24 -> x4, local copies, waits for them, and re-layouts: 5.72 us -> 1.9 us
    pallas_call x1, Pallas kernels: 55.3 us -> 54.1 us  [local(): pl.pallas_call(run, out_shape=[jax.ShapeDtypeStruct((16, 128), F32)] * 2,...]
where the time goes in v2:
time: 57.5 us; the launch traced here: 57.3 us
  Pallas kernels  54.1 us (94%)
  local copies, waits for them, and re-layouts  1.9 us (3%)
  between operations  1.3 us (2%)
    pallas_call x1, Pallas kernels, local(): pl.pallas_call(run, out_shape=[jax.ShapeDtypeStruct((16, 128), F32)] * 2,...  54.1 us
    unnamed x4, local copies, waits for them, and re-layouts  1.9 us

profile of v2, /device:TPU:0, one launch (start us, length us, event | category | flops | bytes accessed | tf_op | source)
XLA Modules:
  0.0 57.3 jit_solution(4936940309469242063)
XLA Ops:
  1.3 54.1 %shard_map.131 = (f32[16,128]{1,0:T(8,128)}, f32[16,128]{1,0:T(8,128)}) custom-call(s32[1,32]{1,0:T(1,128)} %refs_0_.1, s32[1,32]{1,0:T(1,128)} %refs_1_.1, s32[1,1]{1,0:T(1,128)S(6)} %copy.16.refs_2_, f32[16,128]{1,0:T(8,128)} %bitcast.11, f32[16,128]{1,0:T(8,128)} %bitcast.12, bf16[4096,128]{1,0:T(8,128)(2,1)} %bitcast.9, bf16[4,27,32,64]{3,2,1,0:T(8,128)(2,1)} %refs_6_.1, ...), custom_call_target="tpu_custom_call" | custom-call | tf_op jit(solution)/shard_map/pallas_call | solution.py:518
  55.4 0.0 copy-start
  55.4 1.3 %copy.17 = f32[2,8,128]{2,1,0:T(8,128)} copy(f32[2,8,128]{2,1,0:T(8,128)} %bitcast.14) | data formatting | bytes 16384
  56.7 0.0 copy-done
  56.7 0.6 %copy.18 = f32[2,8,128]{2,1,0:T(8,128)} copy(f32[2,8,128]{2,1,0:T(8,128)S(1)} %bitcast.13) | data formatting | bytes 16384
Async XLA Ops:
  55.4 1.3 %copy-start = (f32[16,128]{1,0:T(8,128)S(1)}, f32[16,128]{1,0:T(8,128)}, u32[]{:S(2)}) copy-start(f32[16,128]{1,0:T(8,128)} %get-tuple-element.5) | copy-start | bytes 24580
